TPU v7x, 128 devices: a whole 4x4x4 slice. The times are simulated.
128 devices in a mesh: ctx: 16 (over x, y_lo, core), mp: 8 (over y_hi, z).
Axes of the slice: x: 4, y: 4 (y_hi: 2, y_lo: 2; y = y_hi * 2 + y_lo), z: 4, core: 2. Of those that a mesh axis runs over, the one named last changes fastest.
Arguments:
- prompt_queries: bfloat16 [8192, 8192], P('ctx', 'mp'), may hold values from -21 to 21
- prompt_keys: bfloat16 [8192, 1024], P('ctx', 'mp'), may hold values from -21 to 21
- prompt_values: bfloat16 [8192, 1024], P('ctx', 'mp'), may hold values from -6 to 6
- step_queries: bfloat16 [2, 32, 8192], P(None, 'ctx', 'mp'), may hold values from -21 to 21
- step_keys: bfloat16 [2, 32, 1024], P(None, 'ctx', 'mp'), may hold values from -10 to 10
- step_values: bfloat16 [2, 32, 1024], P(None, 'ctx', 'mp'), may hold values from -6 to 6
- block_owners: int32 [64], P('ctx'), may hold values from 0 to 7, as said below
- prompt_lengths: int32 [4], replicated, may hold values from 512 to 5120, as said below
- row_request: int32 [32], replicated, may hold values from 0 to 3
Outputs:
- prefill_output: bfloat16 [8192, 8192], P('ctx', 'mp')
- owned_keys: bfloat16 [16, 8, 2, 128, 1024], P('ctx', 'mp')
- owned_values: bfloat16 [16, 8, 2, 128, 1024], P('ctx', 'mp')
- decode_output: bfloat16 [2, 32, 8192], P(None, 'ctx', 'mp')
Inputs may be any that keep to these rules, and one draw needn't show every extreme that they name: `block_owners`: among the 4 blocks of one index of ctx, no owner receives more than 2, and in every draw one owner receives exactly 2 blocks from every index of ctx. `prompt_lengths`: the 4 prompts lie end to end; their lengths sum to 8192; exactly one prompt has 5120 tokens.
All inputs are finite; a program needn't handle non-finite values.
Results may differ from a plain program's by a relative error of at most 0.02.
Values may be sent and summed in bfloat16 or wider, within the bound.
A program may use at most 832 MiB of HBM per device.

v0:
```python
import math

import jax
import jax.numpy as jnp
from jax import lax
from jax.sharding import PartitionSpec as P

KVH = 8
HD = 128
BT = 128
STEPS = 2
BLK_DEV = 4
CAP = 2


NEG_FILL = -1e30


def request_of(positions, prompt_lengths):
    endings = jnp.cumsum(prompt_lengths)
    return jnp.sum((positions[:, None] >= endings[None, :]).astype(jnp.int32), axis=1)


def slot_table(owners_run, owner_count):
    block_count = owners_run.shape[0]
    indices = jnp.arange(block_count, dtype=jnp.int32)
    earlier = (owners_run[:, None] == owners_run[None, :]) & (indices[None, :] < indices[:, None])
    slot_index = jnp.sum(earlier.astype(jnp.int32), axis=1)
    target = owners_run * CAP + slot_index
    slot_ids = jnp.arange(owner_count * CAP, dtype=jnp.int32)
    return (target[None, :] == slot_ids[:, None]).astype(jnp.int32)


def empty_state(kv_heads, group_size, row_count):
    return (
        jnp.full((kv_heads, group_size, row_count), NEG_FILL, jnp.float32),
        jnp.zeros((kv_heads, group_size, row_count), jnp.float32),
        jnp.zeros((kv_heads, group_size, row_count, HD), jnp.float32),
    )


def attend(softmax_state, query_block, key_block, value_block, allowed, score_scale):
    highest, totals, running = softmax_state
    scores = (
        jnp.einsum("qhgd,khd->hgqk", query_block, key_block, preferred_element_type=jnp.float32)
        * score_scale
    )
    scores = jnp.where(allowed, scores, NEG_FILL)
    new_high = jnp.maximum(highest, jnp.max(scores, axis=-1))
    fading = jnp.exp(highest - new_high)
    weights = jnp.where(allowed, jnp.exp(scores - new_high[..., None]), 0.0)
    totals = totals * fading + jnp.sum(weights, axis=-1)
    running = running * fading[..., None] + jnp.einsum(
        "hgqk,khd->hgqd",
        weights.astype(jnp.bfloat16),
        value_block,
        preferred_element_type=jnp.float32,
    )
    return (new_high, totals, running)


def on_device(
    prompt_queries,
    prompt_keys,
    prompt_values,
    step_queries,
    step_keys,
    step_values,
    block_owners,
    prompt_lengths,
    row_request,
):
    ctx_count = lax.axis_size("ctx")
    mp_count = lax.axis_size("mp")
    ctx_index = lax.axis_index("ctx")
    mp_index = lax.axis_index("mp")
    local_rows = prompt_queries.shape[0]
    local_heads = prompt_queries.shape[1] // HD
    local_kv = prompt_keys.shape[1] // HD
    group_size = local_heads // local_kv
    score_scale = 1.0 / math.sqrt(HD)
    positions = ctx_index * local_rows + jnp.arange(local_rows, dtype=jnp.int32)
    request = request_of(positions, prompt_lengths)
    query_tiles = prompt_queries.reshape(local_rows, local_kv, group_size, HD)
    dec_rows = step_queries.shape[1]
    own_queries = step_queries.reshape(STEPS, dec_rows, local_kv, group_size, HD)
    initial = (empty_state(local_kv, group_size, local_rows),)
    carried = initial
    first_row = jnp.int32(0)
    key_piece = lax.all_gather(prompt_keys, "ctx", axis=0, tiled=True)
    value_piece = lax.all_gather(prompt_values, "ctx", axis=0, tiled=True)
    piece_rows = key_piece.shape[0]
    for offset in range(0, piece_rows, 256):
        columns = min(256, piece_rows - offset)
        key_block = key_piece[offset : offset + columns].reshape(columns, local_kv, HD)
        value_block = value_piece[offset : offset + columns].reshape(columns, local_kv, HD)
        key_pos = first_row + offset + jnp.arange(columns, dtype=jnp.int32)
        key_request = request_of(key_pos, prompt_lengths)
        allowed = (positions[:, None] >= key_pos[None, :]) & (
            request[:, None] == key_request[None, :]
        )
        prefill_state = attend(
            carried[0], query_tiles, key_block, value_block, allowed, score_scale
        )
        carried = (prefill_state,)
    prefill_totals = carried[0][1]
    prefill_running = carried[0][2]
    prefill_block = prefill_running / prefill_totals[..., None]
    prefill_output = (
        jnp.transpose(prefill_block, (2, 0, 1, 3))
        .reshape(local_rows, local_heads * HD)
        .astype(jnp.bfloat16)
    )
    slot_onehot = slot_table(block_owners, mp_count)
    onehot_bf = slot_onehot.astype(jnp.bfloat16)
    key_blocks = prompt_keys.reshape(BLK_DEV, BT, local_kv * HD)
    value_blocks = prompt_values.reshape(BLK_DEV, BT, local_kv * HD)
    send_keys = (
        jnp.einsum("ob,btd->otd", onehot_bf, key_blocks, preferred_element_type=jnp.float32)
        .astype(jnp.bfloat16)
        .reshape(mp_count, CAP, BT, local_kv * HD)
    )
    send_values = (
        jnp.einsum("ob,btd->otd", onehot_bf, value_blocks, preferred_element_type=jnp.float32)
        .astype(jnp.bfloat16)
        .reshape(mp_count, CAP, BT, local_kv * HD)
    )
    paged_keys, paged_values = (
        lax.all_to_all(send_keys, "mp", split_axis=0, concat_axis=3, tiled=True),
        lax.all_to_all(send_values, "mp", split_axis=0, concat_axis=3, tiled=True),
    )
    owned_keys = paged_keys.reshape(1, 1, CAP, BT, KVH * HD)
    owned_values = paged_values.reshape(1, 1, CAP, BT, KVH * HD)
    fresh_keys = step_keys.reshape(STEPS, dec_rows, local_kv, HD)
    fresh_values = step_values.reshape(STEPS, dec_rows, local_kv, HD)
    step_ids = jnp.arange(STEPS, dtype=jnp.int32)
    step_mask = (step_ids[None, :] <= step_ids[:, None])[None, None, :, None, :]
    head_queries = lax.all_gather(step_queries, "mp", axis=2, tiled=True)
    all_queries = lax.all_gather(head_queries, "ctx", axis=1, tiled=True)
    all_rows = all_queries.shape[1]
    flat_all = all_queries.reshape(STEPS * all_rows, KVH, group_size, HD)
    slot_rows = lax.dynamic_slice_in_dim(slot_onehot, mp_index * CAP, CAP, 0)
    filled = jnp.sum(slot_rows, axis=1) > 0
    block_ids = jnp.sum(slot_rows * jnp.arange(BLK_DEV, dtype=jnp.int32)[None, :], axis=1)
    token_pos = (
        (ctx_index * BLK_DEV + block_ids)[:, None] * BT + jnp.arange(BT, dtype=jnp.int32)[None, :]
    ).reshape(CAP * BT)
    token_live = jnp.broadcast_to(filled[:, None], (CAP, BT)).reshape(CAP * BT)
    token_request = request_of(token_pos, prompt_lengths)
    visible = token_live[None, :] & (
        jnp.tile(row_request, STEPS)[:, None] == token_request[None, :]
    )
    cache_keys = paged_keys.reshape(CAP * BT, KVH, HD)
    cache_values = paged_values.reshape(CAP * BT, KVH, HD)
    head_parts = []
    for kv_head in range(KVH):
        head_parts.append(
            attend(
                empty_state(1, group_size, STEPS * all_rows),
                flat_all[:, kv_head : kv_head + 1],
                cache_keys[:, kv_head : kv_head + 1],
                cache_values[:, kv_head : kv_head + 1],
                visible,
                score_scale,
            )
        )
    partial_value = tuple(
        (
            jnp.concatenate([section[member_index] for section in head_parts], axis=0)
            for member_index in range(3)
        )
    )

    def blocks_of(tensor):
        trailing = tensor.shape[3:]
        reshaped = tensor.reshape(
            (mp_count, local_kv, group_size, STEPS, ctx_count, dec_rows) + trailing
        )
        permuted = (4, 0, 1, 2, 3, 5) + tuple(range(6, 6 + len(trailing)))
        return jnp.transpose(reshaped, permuted)

    global_high = lax.pmax(partial_value[0], ("ctx", "mp"))
    fading = jnp.exp(partial_value[0] - global_high)
    scaled_total = partial_value[1] * fading
    scaled_running = partial_value[2] * fading[..., None]
    leading = ctx_count * mp_count * local_kv
    shares = (
        lax.psum_scatter(
            blocks_of(scaled_total).reshape((leading, group_size, STEPS, dec_rows)),
            ("ctx", "mp"),
            scatter_dimension=0,
            tiled=True,
        ),
        lax.psum_scatter(
            blocks_of(scaled_running).reshape((leading, group_size, STEPS, dec_rows, HD)),
            ("ctx", "mp"),
            scatter_dimension=0,
            tiled=True,
        ),
    )
    picked = (blocks_of(global_high)[ctx_index, mp_index], shares[0], shares[1])
    prompt_high = picked[0]
    scores = (
        jnp.einsum("srhgd,urhd->hgsru", own_queries, fresh_keys, preferred_element_type=jnp.float32)
        * score_scale
    )
    scores = jnp.where(step_mask, scores, NEG_FILL)
    highest = jnp.maximum(prompt_high, jnp.max(scores, axis=-1))
    weights = jnp.where(step_mask, jnp.exp(scores - highest[..., None]), 0.0)
    fading = jnp.exp(prompt_high - highest)
    totals = picked[1] * fading + jnp.sum(weights, axis=-1)
    running = picked[2] * fading[..., None] + jnp.einsum(
        "hgsru,urhd->hgsrd",
        weights.astype(jnp.bfloat16),
        fresh_values,
        preferred_element_type=jnp.float32,
    )
    result = running / totals[..., None]
    decode_output = (
        jnp.transpose(result, (2, 3, 0, 1, 4))
        .reshape(STEPS, dec_rows, local_heads * HD)
        .astype(jnp.bfloat16)
    )
    return (prefill_output, owned_keys, owned_values, decode_output)


def solution(mesh):
    placed = (
        P("ctx", "mp"),
        P("ctx", "mp"),
        P("ctx", "mp"),
        P(None, "ctx", "mp"),
        P(None, "ctx", "mp"),
        P(None, "ctx", "mp"),
        P("ctx"),
        P(),
        P(),
    )
    return jax.shard_map(
        on_device,
        mesh=mesh,
        in_specs=placed,
        out_specs=(
            P("ctx", "mp"),
            P("ctx", "mp", None, None, None),
            P("ctx", "mp", None, None, None),
            P(None, "ctx", "mp"),
        ),
        check_vma=False,
    )
```

profile of v0, /device:TPU:0, one launch (start us, length us, event | category | flops | bytes accessed | tf_op | source)
XLA Modules:
  0.0 908.5 jit_solution(15004580435866588652)
XLA Ops:
  8.0 37.4 %all_gather.14 = bf16[2,2,8192]{2,0,1:T(2,128)(2,1)} all-gather(bf16[2,2,1024]{2,0,1:T(2,128)(2,1)S(1)} %copy.773), channel_id=1, replica_groups=mesh['ctx'=16,'mp'=8] {'mp'}, dimensions={2}, use_global_device_ids=true | all-gather | bytes 73728 | tf_op jit(solution)/shard_map/all_gather | solution.py:138
  50.3 6.4 all-to-all-start.1
  70.5 7.2 all-to-all-start
  83.2 4.3 all-to-all-done
  108.9 62.8 %pmax.7 = f32[8,8,64]{2,1,0:T(8,128)S(1)} all-reduce(f32[8,8,64]{2,1,0:T(8,128)S(1)} %get-tuple-element.154), channel_id=1, replica_groups=mesh['ctx'=16,'mp'=8] {'ctx','mp'}, use_global_device_ids=true, to_apply=%region_110.111 | all-reduce | flops 4096 | bytes 32768 | tf_op jit(solution)/shard_map/pmax | solution.py:182
  177.3 65.2 %all-reduce = f32[128,8,2,2]{1,3,2,0:T(2,128)} all-reduce(f32[128,8,2,2]{1,3,2,0:T(2,128)} %bitcast.1495), channel_id=3, replica_groups=mesh['ctx'=16,'mp'=8] {'ctx','mp'}, use_global_device_ids=true, to_apply=%region_121.122.clone | all-reduce | flops 4096 | bytes 32768
  285.3 4.3 fusion.10
  289.5 3.8 fusion.11
  293.4 3.8 fusion.12
  350.9 3.8 fusion.94
  354.7 3.8 fusion.92
  358.6 3.8 fusion.90
  362.4 3.8 fusion.88
  366.3 4.0 fusion.86
  370.3 3.8 fusion.84
  374.1 3.9 fusion.82
  378.0 3.9 fusion.80
  381.9 3.8 fusion.78
  385.7 3.9 fusion.76
  389.6 3.8 fusion.74
  393.4 3.8 fusion.72
  397.3 3.8 fusion.70
  401.1 3.8 fusion.68
  404.9 3.9 fusion.66
  408.8 4.2 fusion.64
  413.0 3.8 fusion.62
  416.9 3.9 fusion.60
  423.1 4.0 fusion.56
  427.1 3.8 fusion.54
  443.9 3.7 fusion.97
  530.0 20.1 %divide_convert_fusion = bf16[8,512,128]{1,2,0:T(8,128)(2,1)S(1)} fusion(f32[8,512,128]{1,2,0:T(8,128)S(1)} %fusion.97, f32[8,512,128]{1,2,0:T(8,128)S(1)} %fusion.100, f32[8,512,128]{1,2,0:T(8,128)S(1)} %fusion.103, f32[8,512,128]{1,2,0:T(8,128)S(1)} %fusion.106, f32[8,512,128]{1,2,0:T(8,128)S(1)} %fusion.109, f32[8,512,128]{1,2,0:T(8,128)} %fusion.112, ...), kind=kOutput, calls=%fused_computation.225 | convolution fusion | flops 307757056 | bytes 71008256 | tf_op jit(solution)/shard_map/hgqk,khd->hgqd/dot_general | solution.py:53
  551.4 348.8 %reduce-scatter.2.cloned.1.call-done = f32[1,8,2,2,128]{4,1,2,3,0:T(8,128)} async-done(((f32[128,8,2,2,128]{4,1,2,3,0:T(8,128)}), f32[1,8,2,2,128]{4,1,2,3,0:T(8,128)}) %reduce-scatter.2.cloned.1.call-update) | async-done | bytes 16400 | tf_op jit(solution)/shard_map/reduce_scatter | solution.py:194
  (621 shorter events, 246.9 us)
Async XLA Ops:
  7.2 256.1 %copy-start = (bf16[512,1024]{1,0:T(8,128)(2,1)S(1)}, bf16[512,1024]{1,0:T(8,128)(2,1)}, u32[]{:S(2)}) copy-start(bf16[512,1024]{1,0:T(8,128)(2,1)} %param.9) | copy-start | bytes 3145732
  7.2 59.7 %copy-start.209 = (bf16[2,2,128]{2,1,0:T(2,128)(2,1)S(1)}, bf16[2,2,128]{2,1,0:T(2,128)(2,1)}, u32[]{:S(2)}) copy-start(bf16[2,2,128]{2,1,0:T(2,128)(2,1)} %param.13) | copy-start | bytes 3076
  7.2 82.8 %all-gather.8.cloned.1.call-start = ((), (), s32[]{:S(2)}) async-start(), calls=%async_computation.5 | async-start | bytes 1114112 | tf_op jit(solution)/shard_map/all_gather | solution.py:139
  45.5 217.8 %all-gather.4.cloned.1.call-start = ((), (), s32[]{:S(2)}) async-start(), calls=%async_computation.3 | async-start | bytes 2228224 | tf_op jit(solution)/shard_map/all_gather | solution.py:90
  50.3 20.2 %all-to-all-start.1 = ((bf16[8,2,128,128]{3,1,2,0:T(2,128)(2,1)}), bf16[8,2,128,128]{3,1,2,0:T(2,128)(2,1)S(1)}, u32[]{:S(2)}, u32[]{:S(2)}) async-start(bf16[8,2,128,128]{3,1,2,0:T(2,128)(2,1)} %copy.770), calls=%async_computation.1 | async-start | bytes 1048576 | tf_op jit(solution)/shard_map/all_to_all | solution.py:130
  56.7 387.2 %all-gather.6.cloned.1.call-start = ((), (), s32[]{:S(2)}) async-start(), calls=%async_computation.4 | async-start | bytes 2228224 | tf_op jit(solution)/shard_map/all_gather | solution.py:91
  67.0 20.9 %copy-start.203 = (f32[2,2,2,8]{3,1,2,0:T(2,128)}, f32[2,2,2,8]{3,1,2,0:T(2,128)S(1)}, u32[]{:S(2)}) copy-start(f32[2,2,2,8]{3,1,2,0:T(2,128)S(1)} %convolution_multiply_fusion.8) | copy-start | bytes 772
  68.3 20.7 %copy-start.208 = (pred[2,2]{0,1:T(4,128)(4,1)}, pred[2,2]{0,1:T(4,128)(4,1)S(1)}, u32[]{:S(2)}) copy-start(pred[2,2]{0,1:T(4,128)(4,1)S(1)} %iota_compare_fusion.4) | copy-start | bytes 16
  70.5 17.0 %all-to-all-start = ((bf16[8,2,128,128]{3,1,2,0:T(2,128)(2,1)}), bf16[8,2,128,128]{3,1,2,0:T(2,128)(2,1)S(1)}, u32[]{:S(2)}, u32[]{:S(2)}) async-start(bf16[8,2,128,128]{3,1,2,0:T(2,128)(2,1)} %copy.767), calls=%async_computation | async-start | bytes 1048576 | tf_op jit(solution)/shard_map/all_to_all | solution.py:129
  77.7 822.5 %reduce-scatter.2.cloned.1.call-start = ((), (), s32[]{:S(2)}) async-start(), calls=%async_computation.6 | async-start | bytes 2113536 | tf_op jit(solution)/shard_map/reduce_scatter | solution.py:194
  80.6 185.1 %copy-start.52 = (pred[512,256]{0,1:T(8,128)(4,1)}, pred[512,256]{0,1:T(8,128)(4,1)S(1)}, u32[]{:S(2)}) copy-start(pred[512,256]{0,1:T(8,128)(4,1)S(1)} %get-tuple-element.186) | copy-start | bytes 393220
  108.2 147.6 %copy-start.193 = (f32[8,64]{1,0:T(8,128)S(1)}, f32[8,64]{1,0:T(8,128)}, u32[]{:S(2)}) copy-start(f32[8,64]{1,0:T(8,128)} %copy-done.192) | copy-start | bytes 6148
  108.2 146.0 %copy-start.195 = (f32[8,64]{1,0:T(8,128)S(1)}, f32[8,64]{1,0:T(8,128)}, u32[]{:S(2)}) copy-start(f32[8,64]{1,0:T(8,128)} %copy-done.194) | copy-start | bytes 6148
  108.2 144.6 %copy-start.197 = (f32[8,64]{1,0:T(8,128)S(1)}, f32[8,64]{1,0:T(8,128)}, u32[]{:S(2)}) copy-start(f32[8,64]{1,0:T(8,128)} %copy-done.196) | copy-start | bytes 6148
  175.5 81.3 %copy-start.191 = (f32[8,64]{1,0:T(8,128)S(1)}, f32[8,64]{1,0:T(8,128)}, u32[]{:S(2)}) copy-start(f32[8,64]{1,0:T(8,128)} %copy-done.190) | copy-start | bytes 6148
  175.5 81.3 %copy-start.202 = (f32[8,64]{1,0:T(8,128)S(1)}, f32[8,64]{1,0:T(8,128)}, u32[]{:S(2)}) copy-start(f32[8,64]{1,0:T(8,128)} %get-tuple-element.176) | copy-start | bytes 6148
  269.2 173.7 %copy-start.4 = (f32[256,512,8]{1,0,2:T(8,128)}, f32[256,512,8]{1,0,2:T(8,128)S(1)}, u32[]{:S(2)}) copy-start(f32[256,512,8]{1,0,2:T(8,128)S(1)} %get-tuple-element.279) | copy-start | bytes 12582916
  271.2 170.6 %copy-start.6 = (f32[256,512,8]{1,0,2:T(8,128)}, f32[256,512,8]{1,0,2:T(8,128)S(1)}, u32[]{:S(2)}) copy-start(f32[256,512,8]{1,0,2:T(8,128)S(1)} %get-tuple-element.277) | copy-start | bytes 12582916
  273.2 167.5 %copy-start.8 = (f32[256,512,8]{1,0,2:T(8,128)}, f32[256,512,8]{1,0,2:T(8,128)S(1)}, u32[]{:S(2)}) copy-start(f32[256,512,8]{1,0,2:T(8,128)S(1)} %get-tuple-element.275) | copy-start | bytes 12582916
  275.2 164.4 %copy-start.10 = (f32[256,512,8]{1,0,2:T(8,128)}, f32[256,512,8]{1,0,2:T(8,128)S(1)}, u32[]{:S(2)}) copy-start(f32[256,512,8]{1,0,2:T(8,128)S(1)} %get-tuple-element.273) | copy-start | bytes 12582916
  277.2 161.2 %copy-start.12 = (f32[256,512,8]{1,0,2:T(8,128)}, f32[256,512,8]{1,0,2:T(8,128)S(1)}, u32[]{:S(2)}) copy-start(f32[256,512,8]{1,0,2:T(8,128)S(1)} %get-tuple-element.271) | copy-start | bytes 12582916
  279.2 158.1 %copy-start.14 = (f32[256,512,8]{1,0,2:T(8,128)}, f32[256,512,8]{1,0,2:T(8,128)S(1)}, u32[]{:S(2)}) copy-start(f32[256,512,8]{1,0,2:T(8,128)S(1)} %get-tuple-element.269) | copy-start | bytes 12582916
  281.2 155.0 %copy-start.16 = (f32[256,512,8]{1,0,2:T(8,128)}, f32[256,512,8]{1,0,2:T(8,128)S(1)}, u32[]{:S(2)}) copy-start(f32[256,512,8]{1,0,2:T(8,128)S(1)} %get-tuple-element.267) | copy-start | bytes 12582916
  283.2 151.9 %copy-start.18 = (f32[256,512,8]{1,0,2:T(8,128)}, f32[256,512,8]{1,0,2:T(8,128)S(1)}, u32[]{:S(2)}) copy-start(f32[256,512,8]{1,0,2:T(8,128)S(1)} %get-tuple-element.265) | copy-start | bytes 12582916
  285.2 148.1 %copy-start.20 = (f32[256,512,8]{1,0,2:T(8,128)}, f32[256,512,8]{1,0,2:T(8,128)S(1)}, u32[]{:S(2)}) copy-start(f32[256,512,8]{1,0,2:T(8,128)S(1)} %get-tuple-element.263) | copy-start | bytes 12582916
  298.1 122.7 %copy-start.26 = (f32[256,512,8]{1,0,2:T(8,128)}, f32[256,512,8]{1,0,2:T(8,128)S(1)}, u32[]{:S(2)}) copy-start(f32[256,512,8]{1,0,2:T(8,128)S(1)} %get-tuple-element.255) | copy-start | bytes 12582916
  350.9 23.3 %copy-start.138 = (f32[8,512]{1,0:T(8,128)}, f32[8,512]{1,0:T(8,128)S(1)}, u32[]{:S(2)}) copy-start(f32[8,512]{1,0:T(8,128)S(1)} %get-tuple-element.115) | copy-start | bytes 49156
  529.9 370.3 %copy-start.205 = (f32[8,2,2]{0,1,2:T(2,128)S(1)}, f32[8,2,2]{0,1,2:T(2,128)}, u32[]{:S(2)}) copy-start(f32[8,2,2]{0,1,2:T(2,128)} %copy.801) | copy-start | bytes 388
  529.9 370.3 %copy-start.206 = (f32[8,2,2]{0,1,2:T(2,128)S(1)}, f32[8,2,2]{0,1,2:T(2,128)}, u32[]{:S(2)}) copy-start(f32[8,2,2]{0,1,2:T(2,128)} %get-tuple-element.152) | copy-start | bytes 388
  529.9 370.3 %copy-start.207 = (bf16[8,2,2,2]{0,1,3,2:T(2,128)(2,1)S(1)}, bf16[8,2,2,2]{0,1,3,2:T(2,128)(2,1)}, u32[]{:S(2)}) copy-start(bf16[8,2,2,2]{0,1,3,2:T(2,128)(2,1)} %get-tuple-element.150) | copy-start | bytes 388
  530.0 370.3 %copy-start.210 = (bf16[2,2,128]{2,1,0:T(2,128)(2,1)S(1)}, bf16[2,2,128]{2,1,0:T(2,128)(2,1)}, u32[]{:S(2)}) copy-start(bf16[2,2,128]{2,1,0:T(2,128)(2,1)} %param.14) | copy-start | bytes 3076
  530.0 371.8 %copy-start.1 = (bf16[512,1024]{1,0:T(8,128)(2,1)S(1)}, bf16[512,1024]{1,0:T(8,128)(2,1)}, u32[]{:S(2)}) copy-start(bf16[512,1024]{1,0:T(8,128)(2,1)} %param.9) | copy-start | bytes 3145732
  (185 other events, 757.3 us)
Sparse Core Ops, SparseCore 0:
  45.6 33.3 all-gather.7
  80.7 34.0 all-gather.3
  116.5 34.0 all-gather.5
  263.3 636.8 reduce-scatter.1
where the time goes:
time: 918 us; the launch traced here: 908 us
  waiting for transfers between devices  354 us (39%)
  matrix products  204 us (22%)
  blocking collectives  165 us (18%)
  other arithmetic  122 us (13%)
  local copies, waits for them, and re-layouts  33.2 us (4%)
  between operations  16.2 us (2%)
  starting transfers between devices  13.7 us (1%)
    reduce_scatter x1, waiting for transfers between devices, on_device(): lax.psum_scatter(blocks_of(scaled_running).reshape((leading, group_size,...  349 us
    dot_general x40, matrix products, attend(): jnp.einsum('hgqk,khd->hgqd', weights.astype(jnp.bfloat16), value_block, p...  107 us
    reduce_sum x33, other arithmetic, attend(): totals = totals * fading + jnp.sum(weights, axis=-1)  95.5 us
    dot_general x40, matrix products, attend(): jnp.einsum('qhgd,khd->hgqk', query_block, key_block, preferred_element_ty...  93.2 us
    unnamed x1, blocking collectives  65.2 us
    pmax x1, blocking collectives, on_device(): global_high = lax.pmax(partial_value[0], ('ctx', 'mp'))  62.8 us
    all_gather x1, blocking collectives, on_device(): head_queries = lax.all_gather(step_queries, 'mp', axis=2, tiled=True)  37.4 us
  transfers between devices with their start and end apart: 6, of which 2 were waited for; matrix products, arithmetic and copies ran while one was open for 39% of the time, Pallas kernels for 0%

commit v1 on v0

v1 whole, which is shorter than its diff:
```python
import functools
import math

import jax
import jax.numpy as jnp
from jax import lax
from jax.experimental import pallas as pl
from jax.experimental.pallas import tpu as pltpu
from jax.sharding import PartitionSpec as P

HEADS = 8
HD = 128
ROWS = 512
HALF = 256
BT = 128
NBLK = 16
SEQ = NBLK * ROWS
STEP_ROWS = 128
REACH = 10
NEG = -1e30
C = math.log2(math.e) / math.sqrt(HD)
F32 = jnp.float32
BF16 = jnp.bfloat16
MESH = pl.DeviceIdType.MESH
N_MP = 8


def score(queries, keys):
    return lax.dot_general(queries, keys, (((1,), (1,)), ((), ())), preferred_element_type=F32)


def kernel(
    lengths, row_request, owners,
    q_ref, k_ref, v_ref, sq_ref, sk_ref, sv_ref,
    out_ref, dec_ref, pk_ref, pv_ref,
    kv, mk, mq, acc, tot, high, s0, s1, n0, n1, f0, f1, qd, sd, tail, pages_k, pages_v,
    send_sem, recv_sem, psend_sem, precv_sem, self_sem,
):
    ctx = lax.axis_index("ctx")
    mp = lax.axis_index("mp")
    x, y, core = ctx // 4, (ctx // 2) % 2, ctx % 2

    def place(xx, yy, kk):
        return ((xx + 4) % 4) * 4 + yy * 2 + kk

    sib = place(x, y, 1 - core)
    across = place(x, 1 - y, core)
    right = place(x + 1, y, core)
    left = place(x - 1, y, core)

    barrier = pltpu.get_barrier_semaphore()
    for other in (sib, across, right, left):
        pl.semaphore_signal(barrier, inc=1, device_id=(other, mp), device_id_type=MESH)
    for d in range(1, N_MP):
        pl.semaphore_signal(
            barrier, inc=1, device_id=(ctx, (mp + d) % N_MP), device_id_type=MESH
        )

    def rows_of(block):
        return pl.ds(pl.multiple_of(block * ROWS, ROWS), ROWS)

    own = rows_of(ctx)
    kv[own, :HD] = k_ref[...]
    kv[own, HD:] = v_ref[...]
    pl.semaphore_wait(barrier, 4 + N_MP - 1)

    def send(block, to, slot):
        return pltpu.make_async_remote_copy(
            src_ref=kv.at[rows_of(block)],
            dst_ref=kv.at[rows_of(block)],
            send_sem=send_sem.at[slot],
            recv_sem=recv_sem.at[block],
            device_id=(to, mp),
            device_id_type=MESH,
        )

    def arrived(block):
        send(block, sib, 0).wait_recv()

    sent = []

    def forward(block, targets):
        for to in targets:
            copy = send(block, to, len(sent))
            copy.start()
            sent.append(copy)

    forward(ctx, (across, right, left, sib))

    lane = lax.broadcasted_iota(jnp.int32, (1, HD), 1)
    e0 = lengths[0]
    e1 = e0 + lengths[1]
    e2 = e1 + lengths[2]
    begin = jnp.where(lane == 1, e0, jnp.where(lane == 2, e1, jnp.where(lane == 3, e2, 0)))
    end = jnp.where(
        lane == 0, e0, jnp.where(lane == 1, e1, jnp.where(lane == 2, e2, jnp.where(lane == 3, SEQ, 0)))
    )

    def belongs(first, count):
        pos = first + lax.broadcasted_iota(jnp.int32, (count, HD), 0)
        return (pos >= begin) & (pos < end)

    def fill(block, _):
        mk[rows_of(block), :] = jnp.where(belongs(block * ROWS, ROWS), 1.0, 0.0).astype(BF16)
        return 0

    lax.fori_loop(0, NBLK, fill, 0)
    wide = lax.broadcasted_iota(jnp.int32, (ROWS, HD), 1)
    mq[...] = jnp.where(belongs(ctx * ROWS, ROWS) | (wide >= 4), 0.0, NEG).astype(BF16)

    own_of = [owners[b] for b in range(4)]
    slot_of = []
    for b in range(4):
        earlier = jnp.int32(0)
        for a in range(b):
            earlier = earlier + jnp.where(own_of[a] == own_of[b], 1, 0)
        slot_of.append(earlier)

    def fill_page(t, _):
        o, s = t // 2, t % 2
        picked_k = jnp.zeros((BT, HD), F32)
        picked_v = jnp.zeros((BT, HD), F32)
        for b in range(4):
            hit = jnp.where((own_of[b] == o) & (slot_of[b] == s), 1.0, 0.0).astype(F32)
            picked_k = picked_k + hit * k_ref[b * BT : (b + 1) * BT, :].astype(F32)
            picked_v = picked_v + hit * v_ref[b * BT : (b + 1) * BT, :].astype(F32)
        pages_k[o, s] = picked_k.astype(BF16)
        pages_v[o, s] = picked_v.astype(BF16)
        return 0

    lax.fori_loop(0, 2 * N_MP, fill_page, 0)
    mine = pl.ds(pl.multiple_of(mp * HD, HD), HD)
    paged = []
    for d in range(1, N_MP):
        to = (mp + d) % N_MP
        for i, (source, target) in enumerate(((pages_k, pk_ref), (pages_v, pv_ref))):
            copy = pltpu.make_async_remote_copy(
                src_ref=source.at[to],
                dst_ref=target.at[:, :, mine],
                send_sem=psend_sem.at[i, d],
                recv_sem=precv_sem.at[i, d],
                device_id=(ctx, to),
                device_id_type=MESH,
            )
            copy.start()
            paged.append(copy)
    kept = []
    for i, (source, target) in enumerate(((pages_k, pk_ref), (pages_v, pv_ref))):
        copy = pltpu.make_async_copy(source.at[mp], target.at[:, :, mine], self_sem.at[i])
        copy.start()
        kept.append(copy)

    def tile_of(h, half):
        return pl.ds(pl.multiple_of(h * ROWS + half * HALF, HALF), HALF)

    def produce(h, half, blocks, columns, s_ref, n_ref, f_ref, diagonal):
        rows = pl.ds(half * HALF, HALF)
        queries = jnp.concatenate(
            [q_ref[rows, pl.ds(pl.multiple_of(h * HD, HD), HD)], mq[rows, :]], axis=1
        )
        best = None
        for i, block in enumerate(blocks):
            span = pl.ds(pl.multiple_of(block * ROWS, ROWS), columns)
            s = score(queries, jnp.concatenate([kv[span, :HD], mk[span, :]], axis=1))
            if diagonal:
                at = lax.broadcasted_iota(jnp.int32, s.shape, 0) + half * HALF
                s = jnp.where(at >= lax.broadcasted_iota(jnp.int32, s.shape, 1), s, NEG)
            s_ref[:, i * columns : (i + 1) * columns] = s
            for j in range(0, columns, HD):
                part = s[:, j : j + HD]
                best = part if best is None else jnp.maximum(best, part)
        best = jnp.max(best, axis=1, keepdims=True)
        if diagonal:
            n_ref[...] = jnp.broadcast_to(best, (HALF, HD))
        else:
            before = high[tile_of(h, half), :]
            now = jnp.maximum(before, best)
            n_ref[...] = now
            f_ref[...] = jnp.exp2((before - now) * C)

    def consume(h, half, blocks, columns, s_ref, n_ref, f_ref, diagonal):
        at = tile_of(h, half)
        now = n_ref[...]
        total = None
        running = None
        for i, block in enumerate(blocks):
            span = pl.ds(pl.multiple_of(block * ROWS, ROWS), columns)
            parts = []
            for j in range(i * columns, (i + 1) * columns, HD):
                weight = jnp.exp2((s_ref[:, j : j + HD] - now) * C)
                total = weight if total is None else total + weight
                parts.append(weight.astype(BF16))
            product = jnp.dot(
                jnp.concatenate(parts, axis=1), kv[span, HD:], preferred_element_type=F32
            )
            running = product if running is None else running + product
        high[at, :] = now
        if diagonal:
            acc[at, :] = running
            tot[at, :] = total
        else:
            fade = f_ref[...]
            acc[at, :] = acc[at, :] * fade + running
            tot[at, :] = tot[at, :] * fade + total

    def attend(blocks, diagonal=False):
        def stage(work, h, half):
            columns = HALF if diagonal and half == 0 else ROWS
            slot = (s1, n1, f1) if half else (s0, n0, f0)
            work(h, half, blocks, columns, *slot, diagonal)

        stage(produce, 0, 0)

        def body(h, _):
            stage(produce, h, 1)
            stage(consume, h, 0)
            stage(produce, h + 1, 0)
            stage(consume, h, 1)
            return 0

        lax.fori_loop(0, HEADS - 1, body, 0)
        stage(produce, HEADS - 1, 1)
        stage(consume, HEADS - 1, 0)
        stage(consume, HEADS - 1, 1)

    attend((ctx,), diagonal=True)

    chip = ctx // 2

    def nth(n):
        rank = (n - core + 2) // 2 - 1
        near = rank + 1
        swapped = jnp.minimum(rank + 2 - 2 * ((rank + 2) % 2), 5)
        before = jnp.where(y == 1, near, swapped)
        inside = 1 - (n - core + 2) % 2
        return jnp.where((n == 0) & (core == 1), sib, (chip - before) * 2 + inside)

    count = jnp.minimum(ctx, REACH)

    def spot(dx, dy, other_core):
        return place(x + dx, (y + dy) % 2, (core + other_core) % 2)

    def event(dx, dy, targets):
        block = spot(dx, dy, 0)
        arrived(block)
        forward(block, targets + (sib,))

    def mirrored(dx, dy):
        arrived(spot(dx, dy, 1))

    def events(step):
        if step == 0:
            mirrored(0, 0)
            event(0, 1, (right, left))
            event(-1, 0, (right,))
            event(1, 0, ())
            mirrored(0, 1)
            mirrored(-1, 0)
            mirrored(1, 0)
        if step == 1:
            event(1, 1, (left,))
            event(-1, 1, ())
            mirrored(1, 1)
            mirrored(-1, 1)
        if step == 2:
            event(2, 0, ())
            mirrored(2, 0)
        if step == 3:
            event(2, 1, ())
            mirrored(2, 1)

    for step in range(REACH // 2):
        events(step)

        @pl.when(2 * step + 1 < count)
        def _(step=step):
            attend((nth(2 * step), nth(2 * step + 1)))

    @pl.when(count % 2 == 1)
    def _():
        attend((nth(count - 1),))

    def finish(h, _):
        at = pl.ds(pl.multiple_of(h * ROWS, ROWS), ROWS)
        total = jnp.sum(tot[at, :], axis=1, keepdims=True)
        out_ref[:, pl.ds(pl.multiple_of(h * HD, HD), HD)] = (acc[at, :] / total).astype(BF16)
        return 0

    lax.fori_loop(0, HEADS, finish, 0)

    for h in range(HEADS):
        for t in range(2):
            qd[h * 4 + t * 2 : h * 4 + t * 2 + 2, :HD] = sq_ref[
                t, :, h * HD : (h + 1) * HD
            ].astype(F32)
    drow = lax.broadcasted_iota(jnp.int32, (4 * HEADS, HD), 0)
    dlane = lax.broadcasted_iota(jnp.int32, (4 * HEADS, HD), 1)
    drow_t, drow_r = (drow & 3) >> 1, drow & 1
    asked = jnp.where(drow_r == 0, row_request[ctx * 2], row_request[ctx * 2 + 1])
    key_u, key_r = ((dlane - 4) & 3) >> 1, (dlane - 4) & 1
    allowed = ((dlane < 4) & (dlane == asked)) | (
        (dlane >= 4) & (dlane < 8) & (key_r == drow_r) & (key_u <= drow_t)
    )
    qd[:, HD:] = jnp.where(allowed | (dlane > 8), 0.0, NEG)
    queries = qd[...].astype(BF16)
    tail[...] = jnp.zeros_like(tail)
    for t in range(2):
        tail[t * 2 : t * 2 + 2, :HD] = sk_ref[t].astype(F32)
        tail[t * 2 : t * 2 + 2, HD:] = sv_ref[t].astype(F32)
    trow = lax.broadcasted_iota(jnp.int32, (STEP_ROWS, HD), 0)
    tlane = lax.broadcasted_iota(jnp.int32, (STEP_ROWS, HD), 1)
    tmask = jnp.where(tlane == jnp.where(trow < 4, trow + 4, 8), 1.0, 0.0).astype(BF16)
    s = score(queries, jnp.concatenate([tail[:, :HD].astype(BF16), tmask], axis=1))
    sd[:, SEQ:] = s
    best = s
    chunk = 1024
    for k in range(0, SEQ, chunk):
        s = score(queries, jnp.concatenate([kv[k : k + chunk, :HD], mk[k : k + chunk, :]], axis=1))
        sd[:, k : k + chunk] = s
        for j in range(0, chunk, HD):
            best = jnp.maximum(best, s[:, j : j + HD])
    best = jnp.max(best, axis=1, keepdims=True)
    weight = jnp.exp2((sd[:, SEQ:] - best) * C)
    total = weight
    running = jnp.dot(weight.astype(BF16), tail[:, HD:].astype(BF16), preferred_element_type=F32)
    for k in range(0, SEQ, chunk):
        parts = []
        for j in range(k, k + chunk, HD):
            weight = jnp.exp2((sd[:, j : j + HD] - best) * C)
            total = total + weight
            parts.append(weight.astype(BF16))
        running = running + jnp.dot(
            jnp.concatenate(parts, axis=1), kv[k : k + chunk, HD:], preferred_element_type=F32
        )
    result = running / jnp.sum(total, axis=1, keepdims=True)
    for h in range(HEADS):
        for t in range(2):
            dec_ref[t, :, h * HD : (h + 1) * HD] = result[
                h * 4 + t * 2 : h * 4 + t * 2 + 2, :
            ].astype(BF16)

    for copy in sent:
        copy.wait_send()
    for copy in kept:
        copy.wait()
    for copy in paged:
        copy.wait()


def on_device(q, k, v, sq, sk, sv, owners, lengths, row_request):
    vmem = pl.BlockSpec(memory_space=pltpu.VMEM)
    smem = pl.BlockSpec(memory_space=pltpu.SMEM)
    hbm = pl.BlockSpec(memory_space=pl.ANY)
    out, dec, pk, pv = pl.pallas_call(
        kernel,
        out_shape=(
            jax.ShapeDtypeStruct((ROWS, HEADS * HD), BF16),
            jax.ShapeDtypeStruct(sq.shape, BF16),
            jax.ShapeDtypeStruct((2, BT, N_MP * HD), BF16),
            jax.ShapeDtypeStruct((2, BT, N_MP * HD), BF16),
        ),
        in_specs=[smem] * 3 + [vmem] * 6,
        out_specs=(vmem, vmem, hbm, hbm),
        scratch_shapes=[
            pltpu.VMEM((SEQ, 2 * HD), BF16),
            pltpu.VMEM((SEQ, HD), BF16),
            pltpu.VMEM((ROWS, HD), BF16),
            pltpu.VMEM((HEADS * ROWS, HD), F32),
            pltpu.VMEM((HEADS * ROWS, HD), F32),
            pltpu.VMEM((HEADS * ROWS, HD), F32),
            pltpu.VMEM((HALF, 2 * ROWS), F32),
            pltpu.VMEM((HALF, 2 * ROWS), F32),
            pltpu.VMEM((HALF, HD), F32),
            pltpu.VMEM((HALF, HD), F32),
            pltpu.VMEM((HALF, HD), F32),
            pltpu.VMEM((HALF, HD), F32),
            pltpu.VMEM((4 * HEADS, 2 * HD), F32),
            pltpu.VMEM((4 * HEADS, SEQ + STEP_ROWS), F32),
            pltpu.VMEM((STEP_ROWS, 2 * HD), F32),
            pltpu.VMEM((N_MP, 2, BT, HD), BF16),
            pltpu.VMEM((N_MP, 2, BT, HD), BF16),
            pltpu.SemaphoreType.DMA((NBLK,)),
            pltpu.SemaphoreType.DMA((NBLK,)),
            pltpu.SemaphoreType.DMA((2, N_MP)),
            pltpu.SemaphoreType.DMA((2, N_MP)),
            pltpu.SemaphoreType.DMA((2,)),
        ],
        compiler_params=pltpu.CompilerParams(
            collective_id=0, has_side_effects=True, vmem_limit_bytes=56 * 2**20
        ),
        name="prefill_decode",
    )(lengths, row_request, owners, q, k, v, sq, sk, sv)
    shape = (1, 1, 2, BT, N_MP * HD)
    return out, pk.reshape(shape), pv.reshape(shape), dec


def solution(mesh):
    split = P("ctx", "mp")
    steps = P(None, "ctx", "mp")
    paged = P("ctx", "mp", None, None, None)
    return jax.shard_map(
        on_device,
        mesh=mesh,
        in_specs=(split, split, split, steps, steps, steps, P("ctx"), P(), P()),
        out_specs=(split, paged, paged, steps),
        check_vma=False,
    )
```

time: 918 us -> 68.5 us (0.07)
  the two profiles are of different devices: /device:TPU:0 before, /device:TPU:6 now
where the time goes in v1:
time: 68.5 us; the launch traced here: 68.3 us
  Pallas kernels  62.7 us (92%)
  local copies, waits for them, and re-layouts  4.95 us (7%)
    pallas_call x1, Pallas kernels, on_device(): pl.pallas_call(kernel, out_shape=(jax.ShapeDtypeStruct((ROWS, HEADS * HD)...  62.7 us
    unnamed x10, local copies, waits for them, and re-layouts  4.95 us

profile of v1, /device:TPU:6, one launch (start us, length us, event | category | flops | bytes accessed | tf_op | source)
XLA Modules:
  0.0 68.3 jit_solution(5058512401807931428)
XLA Ops:
  0.6 62.7 %prefill_decode.1 = (bf16[512,1024]{1,0:T(8,128)(2,1)}, bf16[2,2,1024]{2,1,0:T(2,128)(2,1)}, bf16[2,128,1024]{2,1,0:T(8,128)(2,1)}, bf16[2,128,1024]{2,1,0:T(8,128)(2,1)}) custom-call(s32[4]{0:T(128)} %lengths.1, s32[32]{0:T(128)} %row_request.1, s32[4]{0:T(128)} %owners.1, bf16[512,1024]{1,0:T(8,128)(2,1)} %q_ref.1, bf16[512,128]{1,0:T(8,128)(2,1)} %k_ref.1, ...), custom_call_target="tpu_custom_call" | custom-call | tf_op jit(solution)/shard_map/prefill_decode/pallas_call | solution.py:354
  63.3 0.0 copy-start.1
  63.3 2.3 %copy.17 = bf16[512,1024]{1,0:T(8,128)(2,1)} copy(bf16[512,1024]{1,0:T(8,128)(2,1)} %get-tuple-element.16) | data formatting | bytes 2097152
  65.6 0.0 copy-done.1
  65.6 0.0 copy-start
  65.6 0.8 %copy.18 = bf16[1,1,2,128,1024]{4,3,2,1,0:T(8,128)(2,1)} copy(bf16[1,1,2,128,1024]{4,3,2,1,0:T(8,128)(2,1)S(1)} %bitcast.3) | data formatting | bytes 1048576
  66.4 0.4 copy-done
  66.9 0.0 copy-start.2
  66.9 0.8 %copy.19 = bf16[1,1,2,128,1024]{4,3,2,1,0:T(8,128)(2,1)} copy(bf16[1,1,2,128,1024]{4,3,2,1,0:T(8,128)(2,1)S(1)} %bitcast.2) | data formatting | bytes 1048576
  67.7 0.0 copy-done.2
  67.7 0.6 copy.20
Async XLA Ops:
  63.3 2.3 %copy-start.1 = (bf16[2,128,1024]{2,1,0:T(8,128)(2,1)S(1)}, bf16[2,128,1024]{2,1,0:T(8,128)(2,1)}, u32[]{:S(2)}) copy-start(bf16[2,128,1024]{2,1,0:T(8,128)(2,1)} %get-tuple-element.9) | copy-start | bytes 1572868
  65.6 1.2 %copy-start = (bf16[2,128,1024]{2,1,0:T(8,128)(2,1)S(1)}, bf16[2,128,1024]{2,1,0:T(8,128)(2,1)}, u32[]{:S(2)}) copy-start(bf16[2,128,1024]{2,1,0:T(8,128)(2,1)} %get-tuple-element.10) | copy-start | bytes 1572868
  66.9 0.8 %copy-start.2 = (bf16[2,2,1024]{2,1,0:T(2,128)(2,1)S(1)}, bf16[2,2,1024]{2,1,0:T(2,128)(2,1)}, u32[]{:S(2)}) copy-start(bf16[2,2,1024]{2,1,0:T(2,128)(2,1)} %get-tuple-element.19) | copy-start | bytes 24580

commit v2 on v1

--- a/solution.py
+++ b/solution.py
@@ -11,7 +11,7 @@
 HEADS = 8
 HD = 128
 ROWS = 512
-HALF = 256
+HALF = ROWS // 2
 BT = 128
 NBLK = 16
 SEQ = NBLK * ROWS
@@ -150,80 +150,86 @@
         copy.start()
         kept.append(copy)
 
-    def tile_of(h, half):
-        return pl.ds(pl.multiple_of(h * ROWS + half * HALF, HALF), HALF)
-
-    def produce(h, half, blocks, columns, s_ref, n_ref, f_ref, diagonal):
-        rows = pl.ds(half * HALF, HALF)
-        queries = jnp.concatenate(
-            [q_ref[rows, pl.ds(pl.multiple_of(h * HD, HD), HD)], mq[rows, :]], axis=1
-        )
-        best = None
-        for i, block in enumerate(blocks):
-            span = pl.ds(pl.multiple_of(block * ROWS, ROWS), columns)
-            s = score(queries, jnp.concatenate([kv[span, :HD], mk[span, :]], axis=1))
-            if diagonal:
-                at = lax.broadcasted_iota(jnp.int32, s.shape, 0) + half * HALF
-                s = jnp.where(at >= lax.broadcasted_iota(jnp.int32, s.shape, 1), s, NEG)
-            s_ref[:, i * columns : (i + 1) * columns] = s
-            for j in range(0, columns, HD):
-                part = s[:, j : j + HD]
-                best = part if best is None else jnp.maximum(best, part)
-        best = jnp.max(best, axis=1, keepdims=True)
-        if diagonal:
-            n_ref[...] = jnp.broadcast_to(best, (HALF, HD))
-        else:
-            before = high[tile_of(h, half), :]
-            now = jnp.maximum(before, best)
-            n_ref[...] = now
-            f_ref[...] = jnp.exp2((before - now) * C)
-
-    def consume(h, half, blocks, columns, s_ref, n_ref, f_ref, diagonal):
-        at = tile_of(h, half)
-        now = n_ref[...]
-        total = None
-        running = None
-        for i, block in enumerate(blocks):
-            span = pl.ds(pl.multiple_of(block * ROWS, ROWS), columns)
-            parts = []
-            for j in range(i * columns, (i + 1) * columns, HD):
-                weight = jnp.exp2((s_ref[:, j : j + HD] - now) * C)
-                total = weight if total is None else total + weight
-                parts.append(weight.astype(BF16))
-            product = jnp.dot(
-                jnp.concatenate(parts, axis=1), kv[span, HD:], preferred_element_type=F32
+    def tile_of(h, first=0, count=ROWS):
+        return pl.ds(pl.multiple_of(h * ROWS + first, HALF), count)
+
+    def bands(diagonal):
+        return ((0, HALF, HALF), (HALF, HALF, ROWS)) if diagonal else ((0, ROWS, ROWS),)
+
+    def produce(h, blocks, s_ref, n_ref, f_ref, diagonal, fresh):
+        for first, count, columns in bands(diagonal):
+            rows = pl.ds(first, count)
+            queries = jnp.concatenate(
+                [q_ref[rows, pl.ds(pl.multiple_of(h * HD, HD), HD)], mq[rows, :]], axis=1
             )
-            running = product if running is None else running + product
-        high[at, :] = now
-        if diagonal:
-            acc[at, :] = running
-            tot[at, :] = total
-        else:
-            fade = f_ref[...]
-            acc[at, :] = acc[at, :] * fade + running
-            tot[at, :] = tot[at, :] * fade + total
-
-    def attend(blocks, diagonal=False):
-        def stage(work, h, half):
-            columns = HALF if diagonal and half == 0 else ROWS
-            slot = (s1, n1, f1) if half else (s0, n0, f0)
-            work(h, half, blocks, columns, *slot, diagonal)
-
-        stage(produce, 0, 0)
-
-        def body(h, _):
-            stage(produce, h, 1)
-            stage(consume, h, 0)
-            stage(produce, h + 1, 0)
-            stage(consume, h, 1)
+            best = None
+            for i, block in enumerate(blocks):
+                span = pl.ds(pl.multiple_of(block * ROWS, ROWS), columns)
+                s = score(queries, jnp.concatenate([kv[span, :HD], mk[span, :]], axis=1))
+                if diagonal:
+                    at = lax.broadcasted_iota(jnp.int32, s.shape, 0) + first
+                    s = jnp.where(at >= lax.broadcasted_iota(jnp.int32, s.shape, 1), s, NEG)
+                s_ref[rows, i * columns : (i + 1) * columns] = s
+                for j in range(0, columns, HD):
+                    part = s[:, j : j + HD]
+                    best = part if best is None else jnp.maximum(best, part)
+            best = jnp.max(best, axis=1, keepdims=True)
+            if fresh:
+                n_ref[rows, :] = jnp.broadcast_to(best, (count, HD))
+            else:
+                before = high[tile_of(h, first, count), :]
+                now = jnp.maximum(before, best)
+                n_ref[rows, :] = now
+                f_ref[rows, :] = jnp.exp2((before - now) * C)
+
+    def consume(h, blocks, s_ref, n_ref, f_ref, diagonal, fresh):
+        for first, count, columns in bands(diagonal):
+            rows = pl.ds(first, count)
+            at = tile_of(h, first, count)
+            now = n_ref[rows, :]
+            total = None
+            running = None
+            for i, block in enumerate(blocks):
+                span = pl.ds(pl.multiple_of(block * ROWS, ROWS), columns)
+                parts = []
+                for j in range(i * columns, (i + 1) * columns, HD):
+                    weight = jnp.exp2((s_ref[rows, j : j + HD] - now) * C)
+                    total = weight if total is None else total + weight
+                    parts.append(weight.astype(BF16))
+                product = jnp.dot(
+                    jnp.concatenate(parts, axis=1), kv[span, HD:], preferred_element_type=F32
+                )
+                running = product if running is None else running + product
+            high[at, :] = now
+            if fresh:
+                acc[at, :] = running
+                tot[at, :] = total
+            else:
+                fade = f_ref[rows, :]
+                acc[at, :] = acc[at, :] * fade + running
+                tot[at, :] = tot[at, :] * fade + total
+
+    def stage(work, h, odd, blocks, diagonal=False, fresh=False):
+        slot = (s1, n1, f1) if odd else (s0, n0, f0)
+        work(h, blocks, *slot, diagonal, fresh)
+
+    def attend(blocks, diagonal=False, fresh=False):
+        kind = (blocks, diagonal, fresh)
+        stage(produce, 0, 0, *kind)
+
+        def body(i, _):
+            stage(produce, 2 * i + 1, 1, *kind)
+            stage(consume, 2 * i, 0, *kind)
+            stage(produce, 2 * i + 2, 0, *kind)
+            stage(consume, 2 * i + 1, 1, *kind)
             return 0
 
-        lax.fori_loop(0, HEADS - 1, body, 0)
-        stage(produce, HEADS - 1, 1)
-        stage(consume, HEADS - 1, 0)
-        stage(consume, HEADS - 1, 1)
-
-    attend((ctx,), diagonal=True)
+        lax.fori_loop(0, HEADS // 2 - 1, body, 0)
+        stage(produce, HEADS - 1, 1, *kind)
+        stage(consume, HEADS - 2, 0, *kind)
+        stage(consume, HEADS - 1, 1, *kind)
+
+    attend((ctx,), diagonal=True, fresh=True)
 
     chip = ctx // 2
 
@@ -269,21 +275,32 @@
             event(2, 1, ())
             mirrored(2, 1)
 
-    for step in range(REACH // 2):
-        events(step)
+    def one_step(step, _):
+        for at in range(4):
+
+            @pl.when(step == at)
+            def _(at=at):
+                events(at)
 
         @pl.when(2 * step + 1 < count)
-        def _(step=step):
+        def _():
             attend((nth(2 * step), nth(2 * step + 1)))
+
+        return 0
+
+    lax.fori_loop(0, REACH // 2, one_step, 0)
 
     @pl.when(count % 2 == 1)
     def _():
         attend((nth(count - 1),))
 
-    def finish(h, _):
+    def finished(h):
         at = pl.ds(pl.multiple_of(h * ROWS, ROWS), ROWS)
         total = jnp.sum(tot[at, :], axis=1, keepdims=True)
-        out_ref[:, pl.ds(pl.multiple_of(h * HD, HD), HD)] = (acc[at, :] / total).astype(BF16)
+        return (acc[at, :] / total).astype(BF16)
+
+    def finish(h, _):
+        out_ref[:, pl.ds(pl.multiple_of(h * HD, HD), HD)] = finished(h)
         return 0
 
     lax.fori_loop(0, HEADS, finish, 0)
@@ -339,12 +356,35 @@
                 h * 4 + t * 2 : h * 4 + t * 2 + 2, :
             ].astype(BF16)
 
-    for copy in sent:
-        copy.wait_send()
+    for slot in range(len(sent)):
+        send(ctx, sib, slot).wait_send()
     for copy in kept:
         copy.wait()
     for copy in paged:
         copy.wait()
+
+
+def copy_kernel(out, pk, pv, dec, out_to, pk_to, pv_to, dec_to, *scratch):
+    held, (sem_in, sem_out) = scratch[:-2], scratch[-2:]
+    parts = []
+    for a, via, b in zip((out, pk, pv, dec), held, (out_to, pk_to, pv_to, dec_to)):
+        for i in range(2):
+            half = a.shape[0] // 2
+            span = pl.ds(i * half, half)
+            n = len(parts)
+            parts.append(
+                (
+                    pltpu.make_async_copy(a.at[span], via.at[span], sem_in.at[n]),
+                    pltpu.make_async_copy(via.at[span], b.at[span], sem_out.at[n]),
+                )
+            )
+    for inward, _ in parts:
+        inward.start()
+    for inward, outward in parts:
+        inward.wait()
+        outward.start()
+    for _, outward in parts:
+        outward.wait()
 
 
 def on_device(q, k, v, sq, sk, sv, owners, lengths, row_request):
@@ -368,12 +408,12 @@
             pltpu.VMEM((HEADS * ROWS, HD), F32),
             pltpu.VMEM((HEADS * ROWS, HD), F32),
             pltpu.VMEM((HEADS * ROWS, HD), F32),
-            pltpu.VMEM((HALF, 2 * ROWS), F32),
-            pltpu.VMEM((HALF, 2 * ROWS), F32),
-            pltpu.VMEM((HALF, HD), F32),
-            pltpu.VMEM((HALF, HD), F32),
-            pltpu.VMEM((HALF, HD), F32),
-            pltpu.VMEM((HALF, HD), F32),
+            pltpu.VMEM((ROWS, 2 * ROWS), F32),
+            pltpu.VMEM((ROWS, 2 * ROWS), F32),
+            pltpu.VMEM((ROWS, HD), F32),
+            pltpu.VMEM((ROWS, HD), F32),
+            pltpu.VMEM((ROWS, HD), F32),
+            pltpu.VMEM((ROWS, HD), F32),
             pltpu.VMEM((4 * HEADS, 2 * HD), F32),
             pltpu.VMEM((4 * HEADS, SEQ + STEP_ROWS), F32),
             pltpu.VMEM((STEP_ROWS, 2 * HD), F32),
@@ -390,6 +430,16 @@
         ),
         name="prefill_decode",
     )(lengths, row_request, owners, q, k, v, sq, sk, sv)
+    results = (out, pk, pv, dec)
+    out, pk, pv, dec = pl.pallas_call(
+        copy_kernel,
+        out_shape=tuple(jax.ShapeDtypeStruct(r.shape, r.dtype) for r in results),
+        in_specs=[hbm] * 4,
+        out_specs=(hbm,) * 4,
+        scratch_shapes=[pltpu.VMEM(r.shape, r.dtype) for r in results]
+        + [pltpu.SemaphoreType.DMA((8,))] * 2,
+        name="results",
+    )(*results)
     shape = (1, 1, 2, BT, N_MP * HD)
     return out, pk.reshape(shape), pv.reshape(shape), dec
 

time: 68.5 us -> 63.5 us (0.927)
  local copies, waits for them, and re-layouts: 4.95 us -> 0 us
    unnamed x10 -> x0, local copies, waits for them, and re-layouts: 4.95 us -> none
    pallas_call x0 -> x1, Pallas kernels: none -> 2.49 us  [on_device(): pl.pallas_call(copy_kernel, out_shape=tuple((jax.ShapeDtypeStruct(r.shape...]
    pallas_call x1, Pallas kernels: 62.7 us -> 60.2 us  [on_device(): pl.pallas_call(kernel, out_shape=(jax.ShapeDtypeStruct((ROWS, HEADS * HD)...]
where the time goes in v2:
time: 63.5 us; the launch traced here: 63.4 us
  Pallas kernels  62.7 us (99%)
  between operations  0.64 us (1%)
    pallas_call x1, Pallas kernels, on_device(): pl.pallas_call(kernel, out_shape=(jax.ShapeDtypeStruct((ROWS, HEADS * HD)...  60.2 us
    pallas_call x1, Pallas kernels, on_device(): pl.pallas_call(copy_kernel, out_shape=tuple((jax.ShapeDtypeStruct(r.shape...  2.49 us

profile of v2, /device:TPU:6, one launch (start us, length us, event | category | flops | bytes accessed | tf_op | source)
XLA Modules:
  0.0 63.4 jit_solution(14074423622494043483)
XLA Ops:
  0.6 60.2 %prefill_decode.1 = (bf16[512,1024]{1,0:T(8,128)(2,1)}, bf16[2,2,1024]{2,1,0:T(2,128)(2,1)}, bf16[2,128,1024]{2,1,0:T(8,128)(2,1)}, bf16[2,128,1024]{2,1,0:T(8,128)(2,1)}) custom-call(s32[4]{0:T(128)} %lengths.1, s32[32]{0:T(128)} %row_request.1, s32[4]{0:T(128)} %owners.1, bf16[512,1024]{1,0:T(8,128)(2,1)} %q_ref.1, bf16[512,128]{1,0:T(8,128)(2,1)} %k_ref.1, ...), custom_call_target="tpu_custom_call" | custom-call | tf_op jit(solution)/shard_map/prefill_decode/pallas_call | solution.py:394
  60.9 2.5 %results.1 = (bf16[512,1024]{1,0:T(8,128)(2,1)}, bf16[2,128,1024]{2,1,0:T(8,128)(2,1)}, bf16[2,128,1024]{2,1,0:T(8,128)(2,1)}, bf16[2,2,1024]{2,1,0:T(2,128)(2,1)}) custom-call(bf16[512,1024]{1,0:T(8,128)(2,1)} %get-tuple-element.12.out, bf16[2,128,1024]{2,1,0:T(8,128)(2,1)} %get-tuple-element.13.pk, bf16[2,128,1024]{2,1,0:T(8,128)(2,1)} %get-tuple-element.14.pv, ...), custom_call_target="tpu_custom_call" | custom-call | tf_op jit(solution)/shard_map/results/pallas_call | solution.py:434

commit v3 on v2

--- a/solution.py
+++ b/solution.py
@@ -31,10 +31,10 @@
 
 def kernel(
     lengths, row_request, owners,
-    q_ref, k_ref, v_ref, sq_ref, sk_ref, sv_ref,
-    out_ref, dec_ref, pk_ref, pv_ref,
-    kv, mk, mq, acc, tot, high, s0, s1, n0, n1, f0, f1, qd, sd, tail, pages_k, pages_v,
-    send_sem, recv_sem, psend_sem, precv_sem, self_sem,
+    q_hbm, k_ref, v_ref, sq_ref, sk_ref, sv_ref,
+    out_hbm, dec_ref, pk_ref, pv_ref,
+    q_ref, out_ref, kv, mk, mq, acc, tot, high, s0, s1, n0, n1, f0, f1, qd, sd, tail, pages_k, pages_v,
+    send_sem, recv_sem, psend_sem, precv_sem, self_sem, ctx_in, mp_in,
 ):
     ctx = lax.axis_index("ctx")
     mp = lax.axis_index("mp")
@@ -49,12 +49,22 @@
     left = place(x - 1, y, core)
 
     barrier = pltpu.get_barrier_semaphore()
-    for other in (sib, across, right, left):
-        pl.semaphore_signal(barrier, inc=1, device_id=(other, mp), device_id_type=MESH)
+    for near in (place(x, 1 - y, 0), place(x + 1, y, 0), place(x - 1, y, 0)):
+        pl.semaphore_signal(barrier, inc=1, device_id=(near, mp), device_id_type=MESH)
     for d in range(1, N_MP):
         pl.semaphore_signal(
-            barrier, inc=1, device_id=(ctx, (mp + d) % N_MP), device_id_type=MESH
+            barrier,
+            inc=1,
+            device_id=(place(x, y, 1), (mp + d) % N_MP),
+            device_id_type=MESH,
         )
+
+    @pl.when(core == 1)
+    def _():
+        pl.semaphore_signal(barrier, inc=1, device_id=(sib, mp), device_id_type=MESH)
+
+    load_q = pltpu.make_async_copy(q_hbm, q_ref, self_sem.at[2])
+    load_q.start()
 
     def rows_of(block):
         return pl.ds(pl.multiple_of(block * ROWS, ROWS), ROWS)
@@ -62,7 +72,19 @@
     own = rows_of(ctx)
     kv[own, :HD] = k_ref[...]
     kv[own, HD:] = v_ref[...]
-    pl.semaphore_wait(barrier, 4 + N_MP - 1)
+
+    def tell(semaphore):
+        pl.semaphore_signal(semaphore, inc=1, device_id=(sib, mp), device_id_type=MESH)
+
+    @pl.when(core == 0)
+    def _():
+        pl.semaphore_wait(barrier, 7)
+        tell(ctx_in)
+
+    @pl.when(core == 1)
+    def _():
+        pl.semaphore_wait(ctx_in, 1)
+
 
     def send(block, to, slot):
         return pltpu.make_async_remote_copy(
@@ -130,22 +152,40 @@
 
     lax.fori_loop(0, 2 * N_MP, fill_page, 0)
     mine = pl.ds(pl.multiple_of(mp * HD, HD), HD)
-    paged = []
-    for d in range(1, N_MP):
-        to = (mp + d) % N_MP
-        for i, (source, target) in enumerate(((pages_k, pk_ref), (pages_v, pv_ref))):
-            copy = pltpu.make_async_remote_copy(
-                src_ref=source.at[to],
-                dst_ref=target.at[:, :, mine],
-                send_sem=psend_sem.at[i, d],
-                recv_sem=precv_sem.at[i, d],
-                device_id=(ctx, to),
-                device_id_type=MESH,
-            )
+    pages = ((pages_k, pk_ref), (pages_v, pv_ref))
+
+    def page_copies():
+        copies = []
+        for d in range(1, N_MP):
+            to = (mp + d) % N_MP
+            for i, (source, target) in enumerate(pages):
+                copies.append(
+                    pltpu.make_async_remote_copy(
+                        src_ref=source.at[to],
+                        dst_ref=target.at[:, :, mine],
+                        send_sem=psend_sem.at[i, d],
+                        recv_sem=precv_sem.at[i, d],
+                        device_id=(ctx, to),
+                        device_id_type=MESH,
+                    )
+                )
+        return copies
+
+    def send_pages():
+        @pl.when(core == 1)
+        def _():
+            pl.semaphore_wait(barrier, 2 * (N_MP - 1))
+            tell(mp_in)
+
+        @pl.when(core == 0)
+        def _():
+            pl.semaphore_wait(mp_in, 1)
+
+        for copy in page_copies():
             copy.start()
-            paged.append(copy)
+
     kept = []
-    for i, (source, target) in enumerate(((pages_k, pk_ref), (pages_v, pv_ref))):
+    for i, (source, target) in enumerate(pages):
         copy = pltpu.make_async_copy(source.at[mp], target.at[:, :, mine], self_sem.at[i])
         copy.start()
         kept.append(copy)
@@ -229,6 +269,7 @@
         stage(consume, HEADS - 2, 0, *kind)
         stage(consume, HEADS - 1, 1, *kind)
 
+    load_q.wait()
     attend((ctx,), diagonal=True, fresh=True)
 
     chip = ctx // 2
@@ -276,19 +317,27 @@
             mirrored(2, 1)
 
     def one_step(step, _):
-        for at in range(4):
+        for at in range(3):
 
             @pl.when(step == at)
             def _(at=at):
                 events(at)
-
-        @pl.when(2 * step + 1 < count)
+                if at == 0:
+                    send_pages()
+                if at == 2:
+                    events(3)
+
+        @pl.when((2 * step + 1 < count) & ((step < 2) | (count < REACH)))
         def _():
             attend((nth(2 * step), nth(2 * step + 1)))
 
         return 0
 
     lax.fori_loop(0, REACH // 2, one_step, 0)
+
+    @pl.when(count == REACH)
+    def _():
+        attend(tuple(nth(n) for n in range(4, REACH)))
 
     @pl.when(count % 2 == 1)
     def _():
@@ -304,6 +353,8 @@
         return 0
 
     lax.fori_loop(0, HEADS, finish, 0)
+    store_out = pltpu.make_async_copy(out_ref, out_hbm, self_sem.at[3])
+    store_out.start()
 
     for h in range(HEADS):
         for t in range(2):
@@ -360,8 +411,9 @@
         send(ctx, sib, slot).wait_send()
     for copy in kept:
         copy.wait()
-    for copy in paged:
+    for copy in page_copies():
         copy.wait()
+    store_out.wait()
 
 
 def copy_kernel(out, pk, pv, dec, out_to, pk_to, pv_to, dec_to, *scratch):
@@ -399,17 +451,19 @@
             jax.ShapeDtypeStruct((2, BT, N_MP * HD), BF16),
             jax.ShapeDtypeStruct((2, BT, N_MP * HD), BF16),
         ),
-        in_specs=[smem] * 3 + [vmem] * 6,
-        out_specs=(vmem, vmem, hbm, hbm),
+        in_specs=[smem] * 3 + [hbm] + [vmem] * 5,
+        out_specs=(hbm, vmem, hbm, hbm),
         scratch_shapes=[
+            pltpu.VMEM((ROWS, HEADS * HD), BF16),
+            pltpu.VMEM((ROWS, HEADS * HD), BF16),
             pltpu.VMEM((SEQ, 2 * HD), BF16),
             pltpu.VMEM((SEQ, HD), BF16),
             pltpu.VMEM((ROWS, HD), BF16),
             pltpu.VMEM((HEADS * ROWS, HD), F32),
             pltpu.VMEM((HEADS * ROWS, HD), F32),
             pltpu.VMEM((HEADS * ROWS, HD), F32),
-            pltpu.VMEM((ROWS, 2 * ROWS), F32),
-            pltpu.VMEM((ROWS, 2 * ROWS), F32),
+            pltpu.VMEM((ROWS, 6 * ROWS), F32),
+            pltpu.VMEM((ROWS, 6 * ROWS), F32),
             pltpu.VMEM((ROWS, HD), F32),
             pltpu.VMEM((ROWS, HD), F32),
             pltpu.VMEM((ROWS, HD), F32),
@@ -423,7 +477,9 @@
             pltpu.SemaphoreType.DMA((NBLK,)),
             pltpu.SemaphoreType.DMA((2, N_MP)),
             pltpu.SemaphoreType.DMA((2, N_MP)),
-            pltpu.SemaphoreType.DMA((2,)),
+            pltpu.SemaphoreType.DMA((4,)),
+            pltpu.SemaphoreType.REGULAR,
+            pltpu.SemaphoreType.REGULAR,
         ],
         compiler_params=pltpu.CompilerParams(
             collective_id=0, has_side_effects=True, vmem_limit_bytes=56 * 2**20

time: 63.5 us -> 56.4 us (0.89)
  the two profiles are of different devices: /device:TPU:6 before, /device:TPU:5 now
where the time goes in v3:
time: 56.4 us; the launch traced here: 56.2 us
  Pallas kernels  55.4 us (98%)
  between operations  0.8 us (1%)
    pallas_call x1, Pallas kernels, on_device(): pl.pallas_call(kernel, out_shape=(jax.ShapeDtypeStruct((ROWS, HEADS * HD)...  52.9 us
    pallas_call x1, Pallas kernels, on_device(): pl.pallas_call(copy_kernel, out_shape=tuple((jax.ShapeDtypeStruct(r.shape...  2.49 us

profile of v3, /device:TPU:5, one launch (start us, length us, event | category | flops | bytes accessed | tf_op | source)
XLA Modules:
  0.0 56.2 jit_solution(5860261460669662934)
XLA Ops:
  0.6 52.9 %prefill_decode.1 = (bf16[512,1024]{1,0:T(8,128)(2,1)}, bf16[2,2,1024]{2,1,0:T(2,128)(2,1)}, bf16[2,128,1024]{2,1,0:T(8,128)(2,1)}, bf16[2,128,1024]{2,1,0:T(8,128)(2,1)}) custom-call(s32[4]{0:T(128)} %lengths.1, s32[32]{0:T(128)} %row_request.1, s32[4]{0:T(128)} %owners.1, bf16[512,1024]{1,0:T(8,128)(2,1)} %q_hbm.1, bf16[512,128]{1,0:T(8,128)(2,1)} %k_ref.1, ...), custom_call_target="tpu_custom_call" | custom-call | tf_op jit(solution)/shard_map/prefill_decode/pallas_call | solution.py:446
  53.6 2.5 %results.1 = (bf16[512,1024]{1,0:T(8,128)(2,1)}, bf16[2,128,1024]{2,1,0:T(8,128)(2,1)}, bf16[2,128,1024]{2,1,0:T(8,128)(2,1)}, bf16[2,2,1024]{2,1,0:T(2,128)(2,1)}) custom-call(bf16[512,1024]{1,0:T(8,128)(2,1)} %get-tuple-element.12.out, bf16[2,128,1024]{2,1,0:T(8,128)(2,1)} %get-tuple-element.13.pk, bf16[2,128,1024]{2,1,0:T(8,128)(2,1)} %get-tuple-element.14.pv, ...), custom_call_target="tpu_custom_call" | custom-call | tf_op jit(solution)/shard_map/results/pallas_call | solution.py:490

commit v4 on v3

--- a/solution.py
+++ b/solution.py
@@ -300,21 +300,45 @@
             mirrored(0, 0)
             event(0, 1, (right, left))
             event(-1, 0, (right,))
+
+            @pl.when(y == 1)
+            def _():
+                mirrored(0, 1)
+
+            @pl.when(y == 0)
+            def _():
+                mirrored(-1, 0)
+
+        if step == 1:
             event(1, 0, ())
-            mirrored(0, 1)
-            mirrored(-1, 0)
-            mirrored(1, 0)
-        if step == 1:
             event(1, 1, (left,))
             event(-1, 1, ())
+
+            @pl.when(y == 1)
+            def _():
+                mirrored(-1, 0)
+
+            @pl.when(y == 0)
+            def _():
+                mirrored(0, 1)
+                mirrored(-1, 1)
+
+        if step == 2:
+            mirrored(1, 0)
             mirrored(1, 1)
-            mirrored(-1, 1)
-        if step == 2:
+
+            @pl.when(y == 1)
+            def _():
+                mirrored(-1, 1)
+
             event(2, 0, ())
             mirrored(2, 0)
         if step == 3:
             event(2, 1, ())
             mirrored(2, 1)
+
+    many = count >= REACH - 1
+    pairs = jnp.where(many, (count - 6) // 2, REACH // 2)
 
     def one_step(step, _):
         for at in range(3):
@@ -327,21 +351,21 @@
                 if at == 2:
                     events(3)
 
-        @pl.when((2 * step + 1 < count) & ((step < 2) | (count < REACH)))
+        @pl.when((2 * step + 1 < count) & (step < pairs))
         def _():
             attend((nth(2 * step), nth(2 * step + 1)))
 
+        @pl.when((count % 2 == 1) & (step == jnp.where(many, 1, 4)))
+        def _():
+            attend((nth(jnp.where(many, 2, count - 1)),))
+
         return 0
 
     lax.fori_loop(0, REACH // 2, one_step, 0)
 
-    @pl.when(count == REACH)
+    @pl.when(many)
     def _():
-        attend(tuple(nth(n) for n in range(4, REACH)))
-
-    @pl.when(count % 2 == 1)
-    def _():
-        attend((nth(count - 1),))
+        attend(tuple(nth(count - 6 + n) for n in range(6)))
 
     def finished(h):
         at = pl.ds(pl.multiple_of(h * ROWS, ROWS), ROWS)
@@ -419,10 +443,12 @@
 def copy_kernel(out, pk, pv, dec, out_to, pk_to, pv_to, dec_to, *scratch):
     held, (sem_in, sem_out) = scratch[:-2], scratch[-2:]
     parts = []
-    for a, via, b in zip((out, pk, pv, dec), held, (out_to, pk_to, pv_to, dec_to)):
-        for i in range(2):
-            half = a.shape[0] // 2
-            span = pl.ds(i * half, half)
+    for a, via, b, count in zip(
+        (out, pk, pv, dec), held, (out_to, pk_to, pv_to, dec_to), (4, 2, 2, 2)
+    ):
+        for i in range(count):
+            size = a.shape[0] // count
+            span = pl.ds(i * size, size)
             n = len(parts)
             parts.append(
                 (
@@ -493,7 +519,7 @@
         in_specs=[hbm] * 4,
         out_specs=(hbm,) * 4,
         scratch_shapes=[pltpu.VMEM(r.shape, r.dtype) for r in results]
-        + [pltpu.SemaphoreType.DMA((8,))] * 2,
+        + [pltpu.SemaphoreType.DMA((10,))] * 2,
         name="results",
     )(*results)
     shape = (1, 1, 2, BT, N_MP * HD)

time: 56.4 us -> 55.4 us (0.982)
  the two profiles are of different devices: /device:TPU:5 before, /device:TPU:6 now
where the time goes in v4:
time: 55.4 us; the launch traced here: 54.6 us
  Pallas kernels  53.8 us (97%)
  between operations  0.8 us (1%)
    pallas_call x1, Pallas kernels, on_device(): pl.pallas_call(kernel, out_shape=(jax.ShapeDtypeStruct((ROWS, HEADS * HD)...  51.3 us
    pallas_call x1, Pallas kernels, on_device(): pl.pallas_call(copy_kernel, out_shape=tuple((jax.ShapeDtypeStruct(r.shape...  2.44 us

profile of v4, /device:TPU:6, one launch (start us, length us, event | category | flops | bytes accessed | tf_op | source)
XLA Modules:
  0.0 54.6 jit_solution(12238060249095928322)
XLA Ops:
  0.6 51.3 %prefill_decode.1 = (bf16[512,1024]{1,0:T(8,128)(2,1)}, bf16[2,2,1024]{2,1,0:T(2,128)(2,1)}, bf16[2,128,1024]{2,1,0:T(8,128)(2,1)}, bf16[2,128,1024]{2,1,0:T(8,128)(2,1)}) custom-call(s32[4]{0:T(128)} %lengths.1, s32[32]{0:T(128)} %row_request.1, s32[4]{0:T(128)} %owners.1, bf16[512,1024]{1,0:T(8,128)(2,1)} %q_hbm.1, bf16[512,128]{1,0:T(8,128)(2,1)} %k_ref.1, ...), custom_call_target="tpu_custom_call" | custom-call | tf_op jit(solution)/shard_map/prefill_decode/pallas_call | solution.py:472
  52.0 2.4 %results.1 = (bf16[512,1024]{1,0:T(8,128)(2,1)}, bf16[2,128,1024]{2,1,0:T(8,128)(2,1)}, bf16[2,128,1024]{2,1,0:T(8,128)(2,1)}, bf16[2,2,1024]{2,1,0:T(2,128)(2,1)}) custom-call(bf16[512,1024]{1,0:T(8,128)(2,1)} %get-tuple-element.12.out, bf16[2,128,1024]{2,1,0:T(8,128)(2,1)} %get-tuple-element.13.pk, bf16[2,128,1024]{2,1,0:T(8,128)(2,1)} %get-tuple-element.14.pv, ...), custom_call_target="tpu_custom_call" | custom-call | tf_op jit(solution)/shard_map/results/pallas_call | solution.py:516
